TPU v7x, 32 devices: a whole 2x2x4 slice. The times are simulated.
32 devices in a mesh: grp: 4 (over z), sub: 8 (over y, x, core).
Axes of the slice: x: 2, y: 2, z: 4, core: 2. Of those that a mesh axis runs over, the one named last changes fastest.
Arguments:
- top_basis: bfloat16 [4, 512, 256], P('grp', 'sub'), may hold values from -0.375 to 0.375
- top_coeffs: bfloat16 [4, 256, 128], P('grp'), may hold values from -6 to 6
- top_coupling: float32 [4, 512, 512], P('grp')
- block_coupling: float32 [4, 8, 128, 512], P('grp', 'sub'), may hold values from -0.09375 to 0.09375
- block_basis: bfloat16 [4, 8, 128, 128], P('grp', 'sub'), may hold values from -0.5 to 0.5
- block_coeffs: bfloat16 [4, 8, 128, 128], P('grp', 'sub'), may hold values from -6 to 6
- sub_basis: bfloat16 [4, 8, 1536, 256], P('grp', 'sub'), may hold values from -0.375 to 0.375
- sub_coeffs: bfloat16 [4, 8, 256, 128], P('grp', 'sub'), may hold values from -6 to 6
- basis_widths: int32 [4, 8], P('grp', 'sub'), may hold values from 32 to 256
- constraint_modes: bfloat16 [4, 8, 1536, 512], P('grp', 'sub'), may hold values from -0.25 to 0.25
- adjacency: int32 [4, 8, 4], P('grp', 'sub'), may hold values from 0 to 4, as said below
Outputs:
- top_values: float32 [4, 512, 128], P('grp')
- block_values: bfloat16 [4, 8, 128, 128], P('grp', 'sub')
- interior: bfloat16 [4, 8, 1536, 128], P('grp', 'sub')
Inputs may be any that keep to these rules, and one draw needn't show every extreme that they name: `adjacency`: the 4 entries of one substructure are different.
All inputs are finite; a program needn't handle non-finite values.
Results may differ from a plain program's by a relative error of at most 0.0044.
Values may be sent and summed in bfloat16 or wider, within the bound.
A program may use at most 64 MiB of HBM per device.

v0:
```python
import jax
import jax.numpy as jnp
from jax import lax
from jax.sharding import PartitionSpec as P


def from_behind(shard, axis, by):
    peers = lax.axis_size(axis)
    return lax.ppermute(shard, axis, [(i, (i + by) % peers) for i in range(peers)])


def from_behind_2(value, axis, steps):
    count = lax.axis_size(axis)
    first, last = (max(0, -steps), min(count, count - steps))
    return lax.ppermute(value, axis, [(source, source + steps) for source in range(first, last)])


def neighbour_block(block, offset):
    return from_behind(block, "sub", -offset)


def run_chain(top_own, chain_matrix):
    highest = lax.Precision.HIGHEST

    def relay(turn_index, current):
        earlier = from_behind_2(current, "grp", 1)
        return top_own + jnp.dot(chain_matrix, earlier, precision=highest)

    return lax.fori_loop(0, lax.axis_size("grp"), relay, jnp.zeros_like(top_own))


def body(
    top_basis,
    top_coeffs,
    top_coupling,
    block_coupling,
    block_basis,
    block_coeffs,
    sub_basis,
    sub_coeffs,
    basis_widths,
    constraint_modes,
    adjacency,
):
    highest = lax.Precision.HIGHEST
    rows_own = jnp.dot(top_basis[0], top_coeffs[0], preferred_element_type=jnp.float32)
    chain_matrix = top_coupling[0]
    column_own = lax.all_to_all(rows_own, "sub", split_axis=1, concat_axis=0, tiled=True)
    column_field = run_chain(column_own, chain_matrix)
    top_field = lax.all_gather(column_field, "sub", axis=1, tiled=True)
    own_block = jnp.dot(block_basis[0, 0], block_coeffs[0, 0], preferred_element_type=jnp.float32)
    from_top = jnp.dot(block_coupling[0, 0], top_field, precision=highest)
    block = (own_block + from_top).astype(jnp.bfloat16)
    records = [block, block, block, block, block]
    for offset in (-2, -1, 1, 2):
        records[offset + 2] = neighbour_block(block, offset)
    candidates = jnp.stack(records)
    slots = adjacency[0, 0]
    chosen = jnp.take(candidates, slots, axis=0)
    linked = chosen.reshape(slots.shape[0] * block.shape[0], block.shape[1])
    bound_part = jnp.dot(constraint_modes[0, 0], linked, preferred_element_type=jnp.float32)
    kept_width = basis_widths[0, 0]
    coeffs = sub_coeffs[0, 0]
    basis = sub_basis[0, 0]
    width_total = coeffs.shape[0]
    live_mask = lax.broadcasted_iota(jnp.int32, (width_total, 1), 0) < kept_width
    live_coeffs = jnp.where(live_mask, coeffs, jnp.zeros_like(coeffs))
    fixed_part = jnp.dot(basis, live_coeffs, preferred_element_type=jnp.float32)
    interior = (fixed_part + bound_part).astype(jnp.bfloat16)
    return (top_field[None], block[None, None], interior[None, None])


def solution(mesh):
    placed = (
        P("grp", "sub", None),
        P("grp", None, None),
        P("grp", None, None),
        P("grp", "sub", None, None),
        P("grp", "sub", None, None),
        P("grp", "sub", None, None),
        P("grp", "sub", None, None),
        P("grp", "sub", None, None),
        P("grp", "sub"),
        P("grp", "sub", None, None),
        P("grp", "sub", None),
    )
    return jax.shard_map(
        body,
        mesh=mesh,
        in_specs=placed,
        out_specs=(P("grp", None, None), P("grp", "sub", None, None), P("grp", "sub", None, None)),
        check_vma=False,
    )
```

profile of v0, /device:TPU:24, one launch (start us, length us, event | category | flops | bytes accessed | tf_op | source)
XLA Modules:
  0.0 61.2 jit_solution(13899152050855184769)
XLA Ops:
  0.7 1.1 %copy.23 = bf16[1,256,128]{1,2,0:T(8,128)(2,1)S(1)} copy(bf16[1,256,128]{2,1,0:T(8,128)(2,1)} %param.14) | data formatting | bytes 131072 | tf_op args[1]
  1.8 0.9 %fusion.17 = f32[8,16,64]{2,1,0:T(8,128)S(1)} fusion(bf16[8,16,256]{2,1,0:T(8,128)(2,1)S(1)} %bitcast.77, bf16[1,64,256]{2,1,0:T(8,128)(2,1)} %param.13), kind=kOutput, calls=%fused_computation.34 | convolution fusion | flops 4194304 | bytes 131072 | tf_op jit(solution)/shard_map/dot_general | solution.py:46
  2.6 0.8 %reshape.99 = f32[8,1,1024]{2,1,0:T(1,128)} reshape(f32[8,16,64]{2,1,0:T(8,128)S(1)} %fusion.17) | data formatting | bytes 65536
  3.4 3.7 %all-to-all-start = ((f32[8,1,1024]{2,1,0:T(1,128)}), f32[8,1,1024]{2,1,0:T(1,128)S(1)}, u32[]{:S(2)}, u32[]{:S(2)}) async-start(f32[8,1,1024]{2,1,0:T(1,128)} %reshape.99), calls=%async_computation | async-start | bytes 65536 | tf_op jit(solution)/shard_map/all_to_all | solution.py:48
  7.8 0.7 %fusion.15 = s32[4]{0:T(128)S(1)} fusion(s32[1,1,4]{2,1,0:T(1,128)} %param.23), kind=kLoop, calls=%fused_computation.32 | loop fusion | flops 12 | bytes 32 | tf_op jit(solution)/shard_map/jit(_take)/jit(_where)/select_n | solution.py:59
  8.4 1.6 %fusion.4 = f32[128,1536]{1,0:T(8,128)S(1)} fusion(bf16[1,1,1536,256]{3,2,1,0:T(8,128)(2,1)} %param.19, bf16[1,1,256,128]{3,2,1,0:T(8,128)(2,1)} %param.20, pred[256]{0:T(512)(128)(4,1)S(1)} %iota_compare_fusion), kind=kOutput, calls=%fused_computation.10 | convolution fusion | flops 100696064 | bytes 1638656 | tf_op jit(solution)/shard_map/dot_general | solution.py:68
  10.1 1.8 %all-to-all-done = f32[8,1,1024]{2,1,0:T(1,128)S(1)} async-done(((f32[8,1,1024]{2,1,0:T(1,128)}), f32[8,1,1024]{2,1,0:T(1,128)S(1)}, u32[]{:S(2)}, u32[]{:S(2)}) %all-to-all-start) | async-done | bytes 32800 | tf_op jit(solution)/shard_map/all_to_all | solution.py:48
  12.5 0.7 %reduce = f32[8,1024]{1,0:T(8,128)S(1)} reduce(f32[8,1,1024]{2,1,0:T(1,128)S(1)} %all-to-all-done, f32[]{:T(128)} %broadcast.83), dimensions={1}, to_apply=%all_to_all.12.reduce_sub_computation | reduce | bytes 65540 | tf_op jit(solution)/shard_map/all_to_all | solution.py:48
  13.4 27.3 %while.11 = (s32[]{:T(128)}, f32[512,16]{0,1:T(8,128)S(1)}, f32[512,512]{1,0:T(8,128)S(1)}, f32[512,16]{0,1:T(8,128)S(1)}, s32[]{:T(128)}, /*index=5*/s32[]{:T(128)}) while((s32[]{:T(128)}, f32[512,16]{0,1:T(8,128)S(1)}, f32[512,512]{1,0:T(8,128)S(1)}, f32[512,16]{0,1:T(8,128)S(1)}, s32[]{:T(128)}, /*index=5*/s32[]{:T(128)}) %tuple.32), condition=%wide.region_1.0_spmd.clone, body=%wide.region_0.0_spmd.clone.sunk | while | flops 50348032 | bytes 1343607 | solution.py:29
  13.4 1.3 %collective-permute-start = (f32[512,16]{0,1:T(8,128)S(1)}, f32[512,16]{0,1:T(8,128)S(1)}, u32[]{:S(2)}, u32[]{:S(2)}) collective-permute-start(f32[512,16]{0,1:T(8,128)S(1)} %broadcast_select_fusion.3), channel_id=1, source_target_pairs={{0,8},{8,16},{16,24},{1,9},{9,17},{17,25},{2,10},{10,18},{18,26},{... | collective-permute-start | bytes 98312 | tf_op jit(solution)/shard_map/while/body/eval_jaxpr/ppermute | solution.py:15
  14.7 4.5 %collective-permute-done = f32[512,16]{0,1:T(8,128)S(1)} collective-permute-done((f32[512,16]{0,1:T(8,128)S(1)}, f32[512,16]{0,1:T(8,128)S(1)}, u32[]{:S(2)}, u32[]{:S(2)}) %collective-permute-start) | collective-permute-done | bytes 32800 | tf_op jit(solution)/shard_map/while/body/eval_jaxpr/ppermute | solution.py:15
  19.2 1.0 %convolution_add_fusion.4 = f32[512,16]{0,1:T(8,128)S(1)} fusion(f32[512,16]{0,1:T(8,128)S(1)} %get-tuple-element.98, f32[512,512]{1,0:T(8,128)S(1)} %get-tuple-element.97, f32[512,16]{0,1:T(8,128)S(1)} %collective-permute-done), kind=kOutput, calls=%fused_computation.1.clone.1 | convolution fusion | flops 50339840 | bytes 1146880 | tf_op jit(solution)/shard_map/while/body/eval_jaxpr/dot_general | solution.py:27
  20.2 1.3 %collective-permute-start = (f32[512,16]{0,1:T(8,128)S(1)}, f32[512,16]{0,1:T(8,128)S(1)}, u32[]{:S(2)}, u32[]{:S(2)}) collective-permute-start(f32[512,16]{0,1:T(8,128)S(1)} %broadcast_select_fusion.3), channel_id=1, source_target_pairs={{0,8},{8,16},{16,24},{1,9},{9,17},{17,25},{2,10},{10,18},{18,26},{... | collective-permute-start | bytes 98312 | tf_op jit(solution)/shard_map/while/body/eval_jaxpr/ppermute | solution.py:15
  21.5 4.5 %collective-permute-done = f32[512,16]{0,1:T(8,128)S(1)} collective-permute-done((f32[512,16]{0,1:T(8,128)S(1)}, f32[512,16]{0,1:T(8,128)S(1)}, u32[]{:S(2)}, u32[]{:S(2)}) %collective-permute-start) | collective-permute-done | bytes 32800 | tf_op jit(solution)/shard_map/while/body/eval_jaxpr/ppermute | solution.py:15
  26.0 1.0 %convolution_add_fusion.4 = f32[512,16]{0,1:T(8,128)S(1)} fusion(f32[512,16]{0,1:T(8,128)S(1)} %get-tuple-element.98, f32[512,512]{1,0:T(8,128)S(1)} %get-tuple-element.97, f32[512,16]{0,1:T(8,128)S(1)} %collective-permute-done), kind=kOutput, calls=%fused_computation.1.clone.1 | convolution fusion | flops 50339840 | bytes 1146880 | tf_op jit(solution)/shard_map/while/body/eval_jaxpr/dot_general | solution.py:27
  27.0 1.3 %collective-permute-start = (f32[512,16]{0,1:T(8,128)S(1)}, f32[512,16]{0,1:T(8,128)S(1)}, u32[]{:S(2)}, u32[]{:S(2)}) collective-permute-start(f32[512,16]{0,1:T(8,128)S(1)} %broadcast_select_fusion.3), channel_id=1, source_target_pairs={{0,8},{8,16},{16,24},{1,9},{9,17},{17,25},{2,10},{10,18},{18,26},{... | collective-permute-start | bytes 98312 | tf_op jit(solution)/shard_map/while/body/eval_jaxpr/ppermute | solution.py:15
  28.3 4.5 %collective-permute-done = f32[512,16]{0,1:T(8,128)S(1)} collective-permute-done((f32[512,16]{0,1:T(8,128)S(1)}, f32[512,16]{0,1:T(8,128)S(1)}, u32[]{:S(2)}, u32[]{:S(2)}) %collective-permute-start) | collective-permute-done | bytes 32800 | tf_op jit(solution)/shard_map/while/body/eval_jaxpr/ppermute | solution.py:15
  32.8 1.0 %convolution_add_fusion.4 = f32[512,16]{0,1:T(8,128)S(1)} fusion(f32[512,16]{0,1:T(8,128)S(1)} %get-tuple-element.98, f32[512,512]{1,0:T(8,128)S(1)} %get-tuple-element.97, f32[512,16]{0,1:T(8,128)S(1)} %collective-permute-done), kind=kOutput, calls=%fused_computation.1.clone.1 | convolution fusion | flops 50339840 | bytes 1146880 | tf_op jit(solution)/shard_map/while/body/eval_jaxpr/dot_general | solution.py:27
  33.9 1.3 %collective-permute-start = (f32[512,16]{0,1:T(8,128)S(1)}, f32[512,16]{0,1:T(8,128)S(1)}, u32[]{:S(2)}, u32[]{:S(2)}) collective-permute-start(f32[512,16]{0,1:T(8,128)S(1)} %broadcast_select_fusion.3), channel_id=1, source_target_pairs={{0,8},{8,16},{16,24},{1,9},{9,17},{17,25},{2,10},{10,18},{18,26},{... | collective-permute-start | bytes 98312 | tf_op jit(solution)/shard_map/while/body/eval_jaxpr/ppermute | solution.py:15
  35.2 4.5 %collective-permute-done = f32[512,16]{0,1:T(8,128)S(1)} collective-permute-done((f32[512,16]{0,1:T(8,128)S(1)}, f32[512,16]{0,1:T(8,128)S(1)}, u32[]{:S(2)}, u32[]{:S(2)}) %collective-permute-start) | collective-permute-done | bytes 32800 | tf_op jit(solution)/shard_map/while/body/eval_jaxpr/ppermute | solution.py:15
  39.7 1.0 %convolution_add_fusion.4 = f32[512,16]{0,1:T(8,128)S(1)} fusion(f32[512,16]{0,1:T(8,128)S(1)} %get-tuple-element.98, f32[512,512]{1,0:T(8,128)S(1)} %get-tuple-element.97, f32[512,16]{0,1:T(8,128)S(1)} %collective-permute-done), kind=kOutput, calls=%fused_computation.1.clone.1 | convolution fusion | flops 50339840 | bytes 1146880 | tf_op jit(solution)/shard_map/while/body/eval_jaxpr/dot_general | solution.py:27
  40.7 8.4 %all_gather.3 = f32[512,128]{0,1:T(8,128)S(1)} all-gather(f32[512,16]{0,1:T(8,128)S(1)} %get-tuple-element.25), channel_id=1, replica_groups=mesh['grp'=4,'sub'=8] {'sub'}, dimensions={1}, use_global_device_ids=true | all-gather | bytes 294912 | tf_op jit(solution)/shard_map/all_gather | solution.py:50
  49.0 1.3 %convolution_bitcast_fusion = f32[128,128]{1,0:T(8,128)S(1)} fusion(f32[512,128]{0,1:T(8,128)S(1)} %all_gather.3, f32[1,1,128,512]{3,2,1,0:T(8,128)} %param.16), kind=kOutput, calls=%fused_computation.8 | convolution fusion | flops 100663296 | bytes 589824 | tf_op jit(solution)/shard_map/dot_general | solution.py:52
  50.4 0.9 %fusion.3 = bf16[128,128]{1,0:T(8,128)(2,1)S(1)} fusion(f32[128,128]{1,0:T(8,128)S(1)} %convolution_bitcast_fusion, bf16[1,1,128,128]{3,2,1,0:T(8,128)(2,1)} %param.18, bf16[1,1,128,128]{3,2,1,0:T(8,128)(2,1)} %param.17), kind=kOutput, calls=%fused_computation.9 | convolution fusion | flops 4227072 | bytes 163840 | tf_op jit(solution)/shard_map/dot_general | solution.py:51
  51.3 1.5 %collective-permute-start.1 = (bf16[128,128]{1,0:T(8,128)(2,1)S(1)}, bf16[128,128]{1,0:T(8,128)(2,1)S(1)}, u32[]{:S(2)}, u32[]{:S(2)}) collective-permute-start(bf16[128,128]{1,0:T(8,128)(2,1)S(1)} %fusion.3), channel_id=1, source_target_pairs={{0,2},{1,3},{2,4},{3,5},{4,6},{5,7},{6,0},{7,1},{8,10},{9,11},{10,... | collective-permute-start | bytes 98312 | tf_op jit(solution)/shard_map/ppermute | solution.py:9
  52.8 1.5 %collective-permute-start.4 = (bf16[128,128]{1,0:T(8,128)(2,1)S(1)}, bf16[128,128]{1,0:T(8,128)(2,1)S(1)}, u32[]{:S(2)}, u32[]{:S(2)}) collective-permute-start(bf16[128,128]{1,0:T(8,128)(2,1)S(1)} %fusion.3), channel_id=1, source_target_pairs={{0,6},{1,7},{2,0},{3,1},{4,2},{5,3},{6,4},{7,5},{8,14},{9,15},{10,... | collective-permute-start | bytes 98312 | tf_op jit(solution)/shard_map/ppermute | solution.py:9
  54.8 0.8 %copy.26 = f32[1,512,128]{2,1,0:T(8,128)} copy(f32[1,512,128]{1,2,0:T(8,128)S(1)} %bitcast.75) | data formatting | bytes 524288
  55.6 0.6 %collective-permute-done.1 = bf16[128,128]{1,0:T(8,128)(2,1)S(1)} collective-permute-done((bf16[128,128]{1,0:T(8,128)(2,1)S(1)}, bf16[128,128]{1,0:T(8,128)(2,1)S(1)}, u32[]{:S(2)}, u32[]{:S(2)}) %collective-permute-start.1) | collective-permute-done | bytes 32800 | tf_op jit(solution)/shard_map/ppermute | solution.py:9
  56.3 2.6 %collective-permute-done.2 = bf16[128,128]{1,0:T(8,128)(2,1)S(1)} collective-permute-done((bf16[128,128]{1,0:T(8,128)(2,1)S(1)}, bf16[128,128]{1,0:T(8,128)(2,1)S(1)}, u32[]{:S(2)}, u32[]{:S(2)}) %collective-permute-start.2) | collective-permute-done | bytes 32800 | tf_op jit(solution)/shard_map/ppermute | solution.py:9
  58.9 0.6 gather_fusion
  59.6 0.7 %fusion.1 = bf16[1,1,1536,128]{2,3,1,0:T(8,128)(2,1)S(1)} fusion(f32[128,1536]{1,0:T(8,128)S(1)} %fusion.4, bf16[512,128]{1,0:T(8,128)(2,1)S(1)} %bitcast.76, bf16[1,1,1536,512]{3,2,1,0:T(8,128)(2,1)S(1)} %copy-done), kind=kOutput, calls=%fused_computation.5 | convolution fusion | flops 201719808 | bytes 2883584 | tf_op jit(solution)/shard_map/dot_general | solution.py:61
  60.3 0.9 %copy.27 = bf16[1,1,1536,128]{3,2,1,0:T(8,128)(2,1)} copy(bf16[1,1,1536,128]{2,3,1,0:T(8,128)(2,1)S(1)} %fusion.1) | data formatting | bytes 786432
  (31 shorter events, 1.4 us)
Async XLA Ops:
  0.6 58.9 %copy-start = (bf16[1,1,1536,512]{3,2,1,0:T(8,128)(2,1)S(1)}, bf16[1,1,1536,512]{3,2,1,0:T(8,128)(2,1)}, u32[]{:S(2)}) copy-start(bf16[1,1,1536,512]{3,2,1,0:T(8,128)(2,1)} %param.22) | copy-start | bytes 4718596
  0.6 9.4 %copy-start.3 = (s32[1,1,4]{2,1,0:T(1,128)S(1)}, s32[1,1,4]{2,1,0:T(1,128)}, u32[]{:S(2)}) copy-start(s32[1,1,4]{2,1,0:T(1,128)} %param.23) | copy-start | bytes 52
  0.7 12.7 %copy-start.1 = (f32[1,512,512]{2,1,0:T(8,128)S(1)}, f32[1,512,512]{2,1,0:T(8,128)}, u32[]{:S(2)}) copy-start(f32[1,512,512]{2,1,0:T(8,128)} %param.15) | copy-start | bytes 3145732
  3.4 8.6 %all-to-all-start = ((f32[8,1,1024]{2,1,0:T(1,128)}), f32[8,1,1024]{2,1,0:T(1,128)S(1)}, u32[]{:S(2)}, u32[]{:S(2)}) async-start(f32[8,1,1024]{2,1,0:T(1,128)} %reshape.99), calls=%async_computation | async-start | bytes 65536 | tf_op jit(solution)/shard_map/all_to_all | solution.py:48
  13.4 5.8 %collective-permute-start = (f32[512,16]{0,1:T(8,128)S(1)}, f32[512,16]{0,1:T(8,128)S(1)}, u32[]{:S(2)}, u32[]{:S(2)}) collective-permute-start(f32[512,16]{0,1:T(8,128)S(1)} %broadcast_select_fusion.3), channel_id=1, source_target_pairs={{0,8},{8,16},{16,24},{1,9},{9,17},{17,25},{2,10},{10,18},{18,26},{... | collective-permute-start | bytes 98312 | tf_op jit(solution)/shard_map/while/body/eval_jaxpr/ppermute | solution.py:15
  20.2 5.8 %collective-permute-start = (f32[512,16]{0,1:T(8,128)S(1)}, f32[512,16]{0,1:T(8,128)S(1)}, u32[]{:S(2)}, u32[]{:S(2)}) collective-permute-start(f32[512,16]{0,1:T(8,128)S(1)} %broadcast_select_fusion.3), channel_id=1, source_target_pairs={{0,8},{8,16},{16,24},{1,9},{9,17},{17,25},{2,10},{10,18},{18,26},{... | collective-permute-start | bytes 98312 | tf_op jit(solution)/shard_map/while/body/eval_jaxpr/ppermute | solution.py:15
  27.0 5.8 %collective-permute-start = (f32[512,16]{0,1:T(8,128)S(1)}, f32[512,16]{0,1:T(8,128)S(1)}, u32[]{:S(2)}, u32[]{:S(2)}) collective-permute-start(f32[512,16]{0,1:T(8,128)S(1)} %broadcast_select_fusion.3), channel_id=1, source_target_pairs={{0,8},{8,16},{16,24},{1,9},{9,17},{17,25},{2,10},{10,18},{18,26},{... | collective-permute-start | bytes 98312 | tf_op jit(solution)/shard_map/while/body/eval_jaxpr/ppermute | solution.py:15
  33.9 5.8 %collective-permute-start = (f32[512,16]{0,1:T(8,128)S(1)}, f32[512,16]{0,1:T(8,128)S(1)}, u32[]{:S(2)}, u32[]{:S(2)}) collective-permute-start(f32[512,16]{0,1:T(8,128)S(1)} %broadcast_select_fusion.3), channel_id=1, source_target_pairs={{0,8},{8,16},{16,24},{1,9},{9,17},{17,25},{2,10},{10,18},{18,26},{... | collective-permute-start | bytes 98312 | tf_op jit(solution)/shard_map/while/body/eval_jaxpr/ppermute | solution.py:15
  51.3 9.0 %copy-start.2 = (bf16[128,128]{1,0:T(8,128)(2,1)}, bf16[128,128]{1,0:T(8,128)(2,1)S(1)}, u32[]{:S(2)}) copy-start(bf16[128,128]{1,0:T(8,128)(2,1)S(1)} %fusion.3) | copy-start | bytes 98308
  51.3 4.9 %collective-permute-start.1 = (bf16[128,128]{1,0:T(8,128)(2,1)S(1)}, bf16[128,128]{1,0:T(8,128)(2,1)S(1)}, u32[]{:S(2)}, u32[]{:S(2)}) collective-permute-start(bf16[128,128]{1,0:T(8,128)(2,1)S(1)} %fusion.3), channel_id=1, source_target_pairs={{0,2},{1,3},{2,4},{3,5},{4,6},{5,7},{6,0},{7,1},{8,10},{9,11},{10,... | collective-permute-start | bytes 98312 | tf_op jit(solution)/shard_map/ppermute | solution.py:9
  52.8 6.1 %collective-permute-start.4 = (bf16[128,128]{1,0:T(8,128)(2,1)S(1)}, bf16[128,128]{1,0:T(8,128)(2,1)S(1)}, u32[]{:S(2)}, u32[]{:S(2)}) collective-permute-start(bf16[128,128]{1,0:T(8,128)(2,1)S(1)} %fusion.3), channel_id=1, source_target_pairs={{0,6},{1,7},{2,0},{3,1},{4,2},{5,3},{6,4},{7,5},{8,14},{9,15},{10,... | collective-permute-start | bytes 98312 | tf_op jit(solution)/shard_map/ppermute | solution.py:9
  54.3 4.6 %collective-permute-start.3 = (bf16[128,128]{1,0:T(8,128)(2,1)S(1)}, bf16[128,128]{1,0:T(8,128)(2,1)S(1)}, u32[]{:S(2)}, u32[]{:S(2)}) collective-permute-start(bf16[128,128]{1,0:T(8,128)(2,1)S(1)} %fusion.3), channel_id=1, source_target_pairs={{0,7},{1,0},{2,1},{3,2},{4,3},{5,4},{6,5},{7,6},{8,15},{9,8},{10,9... | collective-permute-start | bytes 98312 | tf_op jit(solution)/shard_map/ppermute | solution.py:9
  54.3 4.6 %collective-permute-start.2 = (bf16[128,128]{1,0:T(8,128)(2,1)S(1)}, bf16[128,128]{1,0:T(8,128)(2,1)S(1)}, u32[]{:S(2)}, u32[]{:S(2)}) collective-permute-start(bf16[128,128]{1,0:T(8,128)(2,1)S(1)} %fusion.3), channel_id=1, source_target_pairs={{0,1},{1,2},{2,3},{3,4},{4,5},{5,6},{6,7},{7,0},{8,9},{9,10},{10,1... | collective-permute-start | bytes 98312 | tf_op jit(solution)/shard_map/ppermute | solution.py:9
where the time goes:
time: 62.4 us; the launch traced here: 61.2 us
  waiting for transfers between devices  23.1 us (37%)
  starting transfers between devices  12.4 us (20%)
  matrix products  9.37 us (15%)
  blocking collectives  8.37 us (13%)
  local copies, waits for them, and re-layouts  4.93 us (8%)
  other arithmetic  1.54 us (2%)
  between operations  1.47 us (2%)
    ppermute x4, waiting for transfers between devices, from_behind_2(): lax.ppermute(value, axis, [(source, source + steps) for source in range(f...  18 us
    all_gather x1, blocking collectives, body(): top_field = lax.all_gather(column_field, 'sub', axis=1, tiled=True)  8.37 us
    ppermute x4, starting transfers between devices, from_behind_2(): lax.ppermute(value, axis, [(source, source + steps) for source in range(f...  5.17 us
    dot_general x4, matrix products, relay(): return top_own + jnp.dot(chain_matrix, earlier, precision=highest)  3.95 us
    unnamed x17, local copies, waits for them, and re-layouts  3.73 us
    all_to_all x1, starting transfers between devices, body(): lax.all_to_all(rows_own, 'sub', split_axis=1, concat_axis=0, tiled=True)  3.72 us
    ppermute x4, starting transfers between devices, from_behind(): lax.ppermute(shard, axis, [(i, (i + by) % peers) for i in range(peers)])  3.49 us
    ppermute x4, waiting for transfers between devices, from_behind(): lax.ppermute(shard, axis, [(i, (i + by) % peers) for i in range(peers)])  3.21 us
  transfers between devices with their start and end apart: 9, of which 7 were waited for; matrix products, arithmetic and copies ran while one was open for 5% of the time, Pallas kernels for 0%

commit v1 on v0

v1 whole, which is shorter than its diff:
```python
import functools
import jax
import jax.numpy as jnp
from jax import lax
from jax.experimental import pallas as pl
from jax.experimental.pallas import tpu as pltpu
from jax.sharding import PartitionSpec as P

BF16 = jnp.bfloat16
F32 = jnp.float32
NT_DIMS = (((1,), (1,)), ((), ()))


def dot_nt(a, b):
    return lax.dot_general(a, b, NT_DIMS, preferred_element_type=F32)


def kernel(
    groups,
    subs,
    owners,
    tb_hbm,
    tc_hbm,
    c_hbm,
    bc_hbm,
    bb_hbm,
    bk_hbm,
    sb_hbm,
    sc_hbm,
    width_ref,
    cm_hbm,
    adj_ref,
    top_out,
    block_out,
    interior_out,
    tb,
    tc,
    c_in,
    c_hi,
    c_lo,
    bc_in,
    bc_hi,
    bc_lo,
    bb,
    bk,
    own_block,
    sb,
    sc,
    cm,
    fixed,
    pieces,
    gathered_own,
    v_prev,
    v_all,
    top_stage,
    cand,
    linked,
    result,
    in_sem,
    out_sem,
    a2a_send,
    a2a_recv,
    hop_send,
    hop_recv,
    gat_send,
    gat_recv,
    nb_send,
    nb_recv,
):
    g = lax.axis_index("grp")
    s = lax.axis_index("sub")
    rows = tb_hbm.shape[1]
    lane_rows = tb.shape[0]
    per = lane_rows // rows
    chunks = result.shape[0]

    tb[...] = jnp.zeros_like(tb)
    place = pl.multiple_of(lax.rem(s, per) * rows, rows)
    loads = [
        pltpu.make_async_copy(tb_hbm.at[0], tb.at[pl.ds(place, rows)], in_sem.at[0]),
        pltpu.make_async_copy(tc_hbm.at[0], tc, in_sem.at[1]),
        pltpu.make_async_copy(c_hbm.at[0], c_in, in_sem.at[2]),
        pltpu.make_async_copy(bc_hbm.at[0, 0], bc_in, in_sem.at[3]),
        pltpu.make_async_copy(bb_hbm.at[0, 0], bb, in_sem.at[4]),
        pltpu.make_async_copy(bk_hbm.at[0, 0], bk, in_sem.at[5]),
        pltpu.make_async_copy(sb_hbm.at[0, 0], sb, in_sem.at[6]),
        pltpu.make_async_copy(sc_hbm.at[0, 0], sc, in_sem.at[7]),
        pltpu.make_async_copy(cm_hbm.at[0, 0], cm, in_sem.at[8]),
    ]
    for load in loads:
        load.start()

    def peer(d):
        return lax.rem(s + d, subs)

    barrier = pltpu.get_barrier_semaphore()
    for d in range(1, subs):
        pl.semaphore_signal(barrier, 1, device_id=(g, peer(d)), device_id_type=pl.DeviceIdType.MESH)

    @pl.when(g > 0)
    def _():
        pl.semaphore_signal(barrier, 1, device_id=(g - 1, s), device_id_type=pl.DeviceIdType.MESH)

    @pl.when(g < groups - 1)
    def _():
        pl.semaphore_signal(barrier, 1, device_id=(g + 1, s), device_id_type=pl.DeviceIdType.MESH)

    loads[0].wait()
    loads[1].wait()
    own_rows = jnp.dot(tb[...], tc[...], preferred_element_type=F32).T
    pieces[...] = own_rows.reshape(pieces.shape)

    beside = jnp.where(g > 0, 1, 0) + jnp.where(g < groups - 1, 1, 0)
    pl.semaphore_wait(barrier, subs - 1 + beside)

    def remote(src, dst, send, recv, grp, sub):
        return pltpu.make_async_remote_copy(
            src_ref=src,
            dst_ref=dst,
            send_sem=send,
            recv_sem=recv,
            device_id=(grp, sub),
            device_id_type=pl.DeviceIdType.MESH,
        )

    def owner_only(index, action):
        if owners == subs:
            action()
        else:
            pl.when(index < owners)(action)

    def piece_copy(t):
        return remote(pieces.at[t], gathered_own.at[s], a2a_send.at[t], a2a_recv.at[s], g, t)

    for d in range(1, subs):
        t = peer(d)
        owner_only(t, lambda t=t: piece_copy(t).start())

    def keep_own():
        gathered_own[s] = pieces[s]

    owner_only(s, keep_own)

    loads[2].wait()
    c_full = c_in[...]
    high = c_full.astype(BF16)
    c_hi[...] = high
    c_lo[...] = (c_full - high.astype(F32)).astype(BF16)

    def gather_copy(t):
        return remote(v_all.at[s], v_all.at[s], gat_send.at[t], gat_recv.at[s], g, t)

    def hop_copy():
        return remote(v_all.at[s], v_prev, hop_send, hop_recv, g + 1, s)

    def chain():
        for d in range(1, subs):
            src = peer(d)
            remote(pieces.at[0], gathered_own.at[src], a2a_send.at[0], a2a_recv.at[src], g, src).wait_recv()
        parts = []
        for j in range(subs // per):
            total = gathered_own[j * per]
            for k in range(1, per):
                total = total + gathered_own[j * per + k]
            parts.append(total)
        own = jnp.concatenate(parts, axis=1)

        @pl.when(g == 0)
        def _():
            v_all[s] = own.astype(BF16)

        @pl.when(g > 0)
        def _():
            remote(v_all.at[s], v_prev, hop_send, hop_recv, g, s).wait_recv()
            before = v_prev[...]
            v_all[s] = (own + dot_nt(before, c_hi[...]) + dot_nt(before, c_lo[...])).astype(BF16)

        @pl.when(g < groups - 1)
        def _():
            hop_copy().start()

        for d in range(1, subs):
            gather_copy(peer(d)).start()

    loads[3].wait()
    b_full = bc_in[...]
    b_high = b_full.astype(BF16)
    bc_hi[...] = b_high
    bc_lo[...] = (b_full - b_high.astype(F32)).astype(BF16)
    loads[4].wait()
    loads[5].wait()
    own_block[...] = jnp.dot(bb[...], bk[...], preferred_element_type=F32)

    owner_only(s, chain)

    loads[6].wait()
    loads[7].wait()
    coeffs = sc[...]
    live = lax.broadcasted_iota(jnp.int32, coeffs.shape, 0) < width_ref[0, 0]
    coeffs = jnp.where(live, coeffs, jnp.zeros_like(coeffs))
    fixed[...] = jnp.dot(sb[...], coeffs, preferred_element_type=F32)

    def gather_wait(src):
        remote(v_all.at[src], v_all.at[src], gat_send.at[0], gat_recv.at[src], g, src).wait_recv()

    for d in range(1, subs):
        src = peer(d)
        owner_only(src, lambda src=src: gather_wait(src))
    v = v_all[...].reshape(-1, v_all.shape[2])
    block = own_block[...] + dot_nt(bc_hi[...], v) + dot_nt(bc_lo[...], v)
    cand[2] = block.astype(BF16)
    nb_copies = []
    for i, o in enumerate((0, 1, 3, 4)):
        t = lax.rem(s - o + 2 + subs, subs)
        nb_copies.append(remote(cand.at[2], cand.at[o], nb_send.at[i], nb_recv.at[i], g, t))
    for copy in nb_copies:
        copy.start()
    stores = [pltpu.make_async_copy(cand.at[2], block_out.at[0, 0], out_sem.at[chunks])]
    stores[0].start()
    top_stage[...] = v.astype(F32).T
    stores.append(pltpu.make_async_copy(top_stage, top_out.at[0], out_sem.at[chunks + 1]))
    stores[1].start()
    loads[8].wait()
    for copy in nb_copies:
        copy.wait_recv()
    size = cand.shape[1]
    for a in range(linked.shape[0] // size):
        linked[a * size:(a + 1) * size, :] = cand[adj_ref[0, 0, a]]
    step = result.shape[1]
    for i in range(chunks):
        here = slice(i * step, (i + 1) * step)
        bound = jnp.dot(cm[here, :], linked[...], preferred_element_type=F32)
        result[i] = (fixed[here, :] + bound).astype(BF16)
        store = pltpu.make_async_copy(result.at[i], interior_out.at[0, 0, pl.ds(i * step, step)], out_sem.at[i])
        store.start()
        stores.append(store)

    for d in range(1, subs):
        t = peer(d)
        owner_only(t, lambda t=t: piece_copy(t).wait_send())

    def sent():
        @pl.when(g < groups - 1)
        def _():
            hop_copy().wait_send()

        for d in range(1, subs):
            gather_copy(peer(d)).wait_send()

    owner_only(s, sent)
    for copy in nb_copies:
        copy.wait_send()
    for store in stores:
        store.wait()


def body(*args):
    tb, tc, c, bc, bb, bk, sb, sc, widths, cm, adj = args
    groups, subs = lax.axis_size("grp"), lax.axis_size("sub")
    nt, modes = c.shape[1], tc.shape[2]
    rows = tb.shape[1]
    cols = max(16, modes // subs)
    owners = modes // cols
    lane_rows = max(128, rows)
    per = lane_rows // rows
    nb, ni = bc.shape[2], sb.shape[2]
    slots = adj.shape[2]
    chunks = 4
    hbm = pl.BlockSpec(memory_space=pl.ANY)
    smem = pl.BlockSpec(memory_space=pltpu.SMEM)
    dma = pltpu.SemaphoreType.DMA
    vmem = pltpu.VMEM
    scratch = [
        vmem((lane_rows, tb.shape[2]), BF16),
        vmem(tc.shape[1:], BF16),
        vmem((nt, nt), F32),
        vmem((nt, nt), BF16),
        vmem((nt, nt), BF16),
        vmem((nb, nt), F32),
        vmem((nb, nt), BF16),
        vmem((nb, nt), BF16),
        vmem(bb.shape[2:], BF16),
        vmem(bk.shape[2:], BF16),
        vmem((nb, modes), F32),
        vmem(sb.shape[2:], BF16),
        vmem(sc.shape[2:], BF16),
        vmem(cm.shape[2:], BF16),
        vmem((ni, modes), F32),
        vmem((owners, cols, lane_rows), F32),
        vmem((subs, cols, lane_rows), F32),
        vmem((cols, nt), BF16),
        vmem((owners, cols, nt), BF16),
        vmem((nt, modes), F32),
        vmem((5, nb, modes), BF16),
        vmem((slots * nb, modes), BF16),
        vmem((chunks, ni // chunks, modes), BF16),
        dma((9,)),
        dma((chunks + 2,)),
        dma((owners,)),
        dma((subs,)),
        dma,
        dma,
        dma((subs,)),
        dma((owners,)),
        dma((4,)),
        dma((4,)),
    ]
    return pl.pallas_call(
        functools.partial(kernel, groups, subs, owners),
        out_shape=(
            jax.ShapeDtypeStruct((1, nt, modes), F32),
            jax.ShapeDtypeStruct((1, 1, nb, modes), BF16),
            jax.ShapeDtypeStruct((1, 1, ni, modes), BF16),
        ),
        in_specs=[hbm, hbm, hbm, hbm, hbm, hbm, hbm, hbm, smem, hbm, smem],
        out_specs=(hbm, hbm, hbm),
        scratch_shapes=scratch,
        compiler_params=pltpu.CompilerParams(
            collective_id=0, has_side_effects=True, vmem_limit_bytes=60 * 1024 * 1024
        ),
        cost_estimate=pl.CostEstimate(flops=500_000_000, bytes_accessed=5_000_000, transcendentals=0),
    )(*args)


def solution(mesh):
    placed = (
        P("grp", "sub", None),
        P("grp", None, None),
        P("grp", None, None),
        P("grp", "sub", None, None),
        P("grp", "sub", None, None),
        P("grp", "sub", None, None),
        P("grp", "sub", None, None),
        P("grp", "sub", None, None),
        P("grp", "sub"),
        P("grp", "sub", None, None),
        P("grp", "sub", None),
    )
    return jax.shard_map(
        body,
        mesh=mesh,
        in_specs=placed,
        out_specs=(P("grp", None, None), P("grp", "sub", None, None), P("grp", "sub", None, None)),
        check_vma=False,
    )
```

time: 62.4 us -> 30.1 us (0.48); the launches traced: 61.2 us -> 29.8 us
  Pallas kernels: 0 us -> 23.7 us
  waiting for transfers between devices: 23.1 us -> 0 us
  starting transfers between devices: 12.4 us -> 0 us
  matrix products: 9.37 us -> 0 us
  blocking collectives: 8.37 us -> 0 us
  other arithmetic: 1.54 us -> 0 us
    pallas_call x0 -> x1, Pallas kernels: none -> 23.7 us  [body(): pl.pallas_call(functools.partial(kernel, groups, subs, owners), out_shape...]
    ppermute x8 -> x0, waiting for transfers between devices: 21.2 us -> none  [the longest x4 18 us: from_behind_2(): lax.ppermute(value, axis, [(source, source + steps) for source in range(f...]
    dot_general x9 -> x0, matrix products: 9.37 us -> none  [the longest x4 3.95 us: relay(): return top_own + jnp.dot(chain_matrix, earlier, precision=highest)]
    ppermute x8 -> x0, starting transfers between devices: 8.66 us -> none  [the longest x4 5.17 us: from_behind_2(): lax.ppermute(value, axis, [(source, source + steps) for source in range(f...]
    all_gather x1 -> x0, blocking collectives: 8.37 us -> none  [body(): top_field = lax.all_gather(column_field, 'sub', axis=1, tiled=True)]
    all_to_all x1 -> x0, starting transfers between devices: 3.72 us -> none  [body(): lax.all_to_all(rows_own, 'sub', split_axis=1, concat_axis=0, tiled=True)]
    all_to_all x1 -> x0, waiting for transfers between devices: 1.83 us -> none  [body(): lax.all_to_all(rows_own, 'sub', split_axis=1, concat_axis=0, tiled=True)]
    unnamed x17 -> x3, local copies, waits for them, and re-layouts: 3.73 us -> 4.81 us
  transfers between devices with their start and end apart: 9 -> 0, of which waited for: 7 -> 0; matrix products, arithmetic and copies ran while one was open for 5% -> 0% of each run, Pallas kernels for 0% -> 0%
where the time goes in v1:
time: 30.1 us; the launch traced here: 29.8 us
  Pallas kernels  23.7 us (79%)
  local copies, waits for them, and re-layouts  4.81 us (16%)
  between operations  1.29 us (4%)
    pallas_call x1, Pallas kernels, body(): pl.pallas_call(functools.partial(kernel, groups, subs, owners), out_shape...  23.7 us
    unnamed x3, local copies, waits for them, and re-layouts  4.81 us

profile of v1, /device:TPU:24, one launch (start us, length us, event | category | flops | bytes accessed | tf_op | source)
XLA Modules:
  0.0 29.8 jit_solution(3285510881641337780)
XLA Ops:
  1.3 23.7 %shard_map.130 = (f32[1,512,128]{2,1,0:T(8,128)}, bf16[1,1,128,128]{3,2,1,0:T(8,128)(2,1)}, bf16[1,1,1536,128]{3,2,1,0:T(8,128)(2,1)}) custom-call(bf16[1,64,256]{2,1,0:T(8,128)(2,1)} %tb_hbm.1, bf16[1,256,128]{2,1,0:T(8,128)(2,1)} %tc_hbm.1, f32[1,512,512]{2,1,0:T(8,128)} %c_hbm.1, f32[1,1,128,512]{3,2,1,0:T(8,128)} %bc_hbm.1, ...), custom_call_target="tpu_custom_call" | custom-call | flops 500000000 | bytes 5000000 | tf_op jit(solution)/shard_map/pallas_call | solution.py:308
  25.0 1.7 %copy.18 = f32[1,512,128]{2,1,0:T(8,128)} copy(f32[1,512,128]{2,1,0:T(8,128)} %get-tuple-element.6) | data formatting | bytes 524288
  26.7 1.4 %copy.19 = bf16[1,1,128,128]{3,2,1,0:T(8,128)(2,1)} copy(bf16[1,1,128,128]{3,2,1,0:T(8,128)(2,1)} %get-tuple-element.7) | data formatting | bytes 65536
  28.0 1.8 %copy.20 = bf16[1,1,1536,128]{3,2,1,0:T(8,128)(2,1)} copy(bf16[1,1,1536,128]{3,2,1,0:T(8,128)(2,1)} %get-tuple-element.8) | data formatting | bytes 786432

commit v2 on v1

--- a/solution.py
+++ b/solution.py
@@ -254,6 +254,32 @@
         store.wait()
 
 
+def hand_over_kernel(top, block, interior, top_out, block_out, interior_out, sem):
+    copies = []
+    half = interior.shape[2] // 2
+    pairs = [(top, top_out), (block, block_out)]
+    for i in range(2):
+        part = (0, 0, pl.ds(i * half, half))
+        pairs.append((interior.at[part], interior_out.at[part]))
+    for i, (source, target) in enumerate(pairs):
+        copies.append(pltpu.make_async_copy(source, target, sem.at[i]))
+        copies[-1].start()
+    for copy in copies:
+        copy.wait()
+
+
+def hand_over(results):
+    hbm = pl.BlockSpec(memory_space=pl.ANY)
+    return pl.pallas_call(
+        hand_over_kernel,
+        out_shape=tuple(jax.ShapeDtypeStruct(r.shape, r.dtype) for r in results),
+        in_specs=[hbm] * 3,
+        out_specs=(hbm,) * 3,
+        scratch_shapes=[pltpu.SemaphoreType.DMA((4,))],
+        compiler_params=pltpu.CompilerParams(vmem_limit_bytes=8 * 1024 * 1024),
+    )(*results)
+
+
 def body(*args):
     tb, tc, c, bc, bb, bk, sb, sc, widths, cm, adj = args
     groups, subs = lax.axis_size("grp"), lax.axis_size("sub")
@@ -305,7 +331,7 @@
         dma((4,)),
         dma((4,)),
     ]
-    return pl.pallas_call(
+    results = pl.pallas_call(
         functools.partial(kernel, groups, subs, owners),
         out_shape=(
             jax.ShapeDtypeStruct((1, nt, modes), F32),
@@ -316,10 +342,11 @@
         out_specs=(hbm, hbm, hbm),
         scratch_shapes=scratch,
         compiler_params=pltpu.CompilerParams(
-            collective_id=0, has_side_effects=True, vmem_limit_bytes=60 * 1024 * 1024
+            collective_id=0, has_side_effects=True, vmem_limit_bytes=24 * 1024 * 1024
         ),
         cost_estimate=pl.CostEstimate(flops=500_000_000, bytes_accessed=5_000_000, transcendentals=0),
-    )(*args)
+    )(*[pltpu.with_memory_space_constraint(a, pltpu.HBM) if a.ndim > 2 and a.dtype != jnp.int32 else a for a in args])
+    return hand_over(results)
 
 
 def solution(mesh):

time: 30.1 us -> 27 us (0.90)
  local copies, waits for them, and re-layouts: 4.81 us -> 0.65 us
  Pallas kernels: 23.7 us -> 24.9 us
    unnamed x3 -> x2, local copies, waits for them, and re-layouts: 4.81 us -> 0.65 us
    pallas_call x0 -> x1, Pallas kernels: none -> 0.88 us  [hand_over(): pl.pallas_call(hand_over_kernel, out_shape=tuple((jax.ShapeDtypeStruct(r....]
    pallas_call x1, Pallas kernels: 23.7 us -> 24 us  [body(): pl.pallas_call(functools.partial(kernel, groups, subs, owners), out_shape...]
where the time goes in v2:
time: 27 us; the launch traced here: 26.9 us
  Pallas kernels  24.9 us (92%)
  between operations  1.3 us (5%)
  local copies, waits for them, and re-layouts  0.65 us (2%)
    pallas_call x1, Pallas kernels, body(): pl.pallas_call(functools.partial(kernel, groups, subs, owners), out_shape...  24 us
    pallas_call x1, Pallas kernels, hand_over(): pl.pallas_call(hand_over_kernel, out_shape=tuple((jax.ShapeDtypeStruct(r....  0.88 us
    unnamed x2, local copies, waits for them, and re-layouts  0.65 us

profile of v2, /device:TPU:24, one launch (start us, length us, event | category | flops | bytes accessed | tf_op | source)
XLA Modules:
  0.0 26.9 jit_solution(1828702571618244477)
XLA Ops:
  1.3 0.0 copy-start
  1.3 0.6 %copy-done = s32[1,1,4]{2,1,0:T(1,128)S(1)} copy-done((s32[1,1,4]{2,1,0:T(1,128)S(1)}, s32[1,1,4]{2,1,0:T(1,128)}, u32[]{:S(2)}) %copy-start) | copy-done | bytes 40
  1.9 24.0 %shard_map.130 = (f32[1,512,128]{2,1,0:T(8,128)S(1)}, bf16[1,1,128,128]{3,2,1,0:T(8,128)(2,1)S(1)}, bf16[1,1,1536,128]{3,2,1,0:T(8,128)(2,1)S(1)}) custom-call(bf16[1,64,256]{2,1,0:T(8,128)(2,1)} %tb_hbm.1, bf16[1,256,128]{2,1,0:T(8,128)(2,1)} %tc_hbm.1, f32[1,512,512]{2,1,0:T(8,128)} %c_hbm.1, f32[1,1,128,512]{3,2,1,0:T(8,128)} %bc_hbm.1, ...), custom_call_target="tpu_custom_call" | custom-call | flops 500000000 | bytes 5000000 | tf_op jit(solution)/shard_map/pallas_call | solution.py:334
  26.0 0.9 %shard_map.131 = (f32[1,512,128]{2,1,0:T(8,128)}, bf16[1,1,128,128]{3,2,1,0:T(8,128)(2,1)}, bf16[1,1,1536,128]{3,2,1,0:T(8,128)(2,1)}) custom-call(f32[1,512,128]{2,1,0:T(8,128)S(1)} %get-tuple-element.6.top, bf16[1,1,128,128]{3,2,1,0:T(8,128)(2,1)S(1)} %get-tuple-element.7.block, bf16[1,1,1536,128]{3,2,1,0:T(8,128)(2,1)S(1)} %get-tuple-element.8.interior), custom_call_target="tpu_custom_call" | custom-call | tf_op jit(solution)/shard_map/pallas_call | solution.py:273
Async XLA Ops:
  1.3 0.7 %copy-start = (s32[1,1,4]{2,1,0:T(1,128)S(1)}, s32[1,1,4]{2,1,0:T(1,128)}, u32[]{:S(2)}) copy-start(s32[1,1,4]{2,1,0:T(1,128)} %adj_ref.1) | copy-start | bytes 52

commit v3 on v2

--- a/solution.py
+++ b/solution.py
@@ -66,6 +66,9 @@
     gat_recv,
     nb_send,
     nb_recv,
+    gathered_before,
+    ahead_send,
+    ahead_recv,
 ):
     g = lax.axis_index("grp")
     s = lax.axis_index("sub")
@@ -97,20 +100,30 @@
     for d in range(1, subs):
         pl.semaphore_signal(barrier, 1, device_id=(g, peer(d)), device_id_type=pl.DeviceIdType.MESH)
 
-    @pl.when(g > 0)
+    def greet(grp, sub):
+        pl.semaphore_signal(barrier, 1, device_id=(grp, sub), device_id_type=pl.DeviceIdType.MESH)
+
+    @pl.when(g < min(groups, 2))
     def _():
-        pl.semaphore_signal(barrier, 1, device_id=(g - 1, s), device_id_type=pl.DeviceIdType.MESH)
-
-    @pl.when(g < groups - 1)
+        if groups > 1:
+            for d in range(subs):
+                greet(1 - g, peer(d))
+
+    @pl.when(g > 1)
     def _():
-        pl.semaphore_signal(barrier, 1, device_id=(g + 1, s), device_id_type=pl.DeviceIdType.MESH)
+        greet(g - 1, s)
+
+    @pl.when((g > 0) & (g < groups - 1))
+    def _():
+        greet(g + 1, s)
 
     loads[0].wait()
     loads[1].wait()
     own_rows = jnp.dot(tb[...], tc[...], preferred_element_type=F32).T
     pieces[...] = own_rows.reshape(pieces.shape)
 
-    beside = jnp.where(g > 0, 1, 0) + jnp.where(g < groups - 1, 1, 0)
+    front = subs if groups > 1 else 0
+    beside = jnp.where(g > 1, 1, front) + jnp.where((g > 0) & (g < groups - 1), 1, 0)
     pl.semaphore_wait(barrier, subs - 1 + beside)
 
     def remote(src, dst, send, recv, grp, sub):
@@ -132,6 +145,16 @@
     def piece_copy(t):
         return remote(pieces.at[t], gathered_own.at[s], a2a_send.at[t], a2a_recv.at[s], g, t)
 
+    def ahead_copy(t):
+        return remote(pieces.at[t], gathered_before.at[s], ahead_send.at[t], ahead_recv.at[s], 1, t)
+
+    if groups > 1:
+        @pl.when(g == 0)
+        def _():
+            for d in range(subs):
+                t = peer(d)
+                owner_only(t, lambda t=t: ahead_copy(t).start())
+
     for d in range(1, subs):
         t = peer(d)
         owner_only(t, lambda t=t: piece_copy(t).start())
@@ -141,64 +164,85 @@
 
     owner_only(s, keep_own)
 
-    loads[2].wait()
-    c_full = c_in[...]
-    high = c_full.astype(BF16)
-    c_hi[...] = high
-    c_lo[...] = (c_full - high.astype(F32)).astype(BF16)
-
     def gather_copy(t):
         return remote(v_all.at[s], v_all.at[s], gat_send.at[t], gat_recv.at[s], g, t)
 
     def hop_copy():
         return remote(v_all.at[s], v_prev, hop_send, hop_recv, g + 1, s)
+
+    def collect(ref):
+        parts = []
+        for j in range(subs // per):
+            total = ref[j * per]
+            for k in range(1, per):
+                total = total + ref[j * per + k]
+            parts.append(total)
+        return jnp.concatenate(parts, axis=1)
 
     def chain():
         for d in range(1, subs):
             src = peer(d)
             remote(pieces.at[0], gathered_own.at[src], a2a_send.at[0], a2a_recv.at[src], g, src).wait_recv()
-        parts = []
-        for j in range(subs // per):
-            total = gathered_own[j * per]
-            for k in range(1, per):
-                total = total + gathered_own[j * per + k]
-            parts.append(total)
-        own = jnp.concatenate(parts, axis=1)
+        own = collect(gathered_own)
 
         @pl.when(g == 0)
         def _():
             v_all[s] = own.astype(BF16)
 
+        @pl.when(g == 1)
+        def _():
+            for d in range(subs):
+                src = peer(d)
+                remote(pieces.at[0], gathered_before.at[src], ahead_send.at[0], ahead_recv.at[src], g, src).wait_recv()
+            v_prev[...] = collect(gathered_before).astype(BF16)
+
+        @pl.when(g > 1)
+        def _():
+            remote(v_all.at[s], v_prev, hop_send, hop_recv, g, s).wait_recv()
+
         @pl.when(g > 0)
         def _():
-            remote(v_all.at[s], v_prev, hop_send, hop_recv, g, s).wait_recv()
             before = v_prev[...]
-            v_all[s] = (own + dot_nt(before, c_hi[...]) + dot_nt(before, c_lo[...])).astype(BF16)
-
-        @pl.when(g < groups - 1)
+            v_all[s] = (own + jnp.dot(before, c_hi[...], preferred_element_type=F32) + jnp.dot(before, c_lo[...], preferred_element_type=F32)).astype(BF16)
+
+        @pl.when((g > 0) & (g < groups - 1))
         def _():
             hop_copy().start()
 
         for d in range(1, subs):
             gather_copy(peer(d)).start()
 
-    loads[3].wait()
-    b_full = bc_in[...]
-    b_high = b_full.astype(BF16)
-    bc_hi[...] = b_high
-    bc_lo[...] = (b_full - b_high.astype(F32)).astype(BF16)
-    loads[4].wait()
-    loads[5].wait()
-    own_block[...] = jnp.dot(bb[...], bk[...], preferred_element_type=F32)
+    def local_work():
+        loads[3].wait()
+        b_full = bc_in[...]
+        b_high = b_full.astype(BF16)
+        bc_hi[...] = b_high
+        bc_lo[...] = (b_full - b_high.astype(F32)).astype(BF16)
+        loads[4].wait()
+        loads[5].wait()
+        own_block[...] = jnp.dot(bb[...], bk[...], preferred_element_type=F32)
+        loads[6].wait()
+        loads[7].wait()
+        coeffs = sc[...]
+        live = lax.broadcasted_iota(jnp.int32, coeffs.shape, 0) < width_ref[0, 0]
+        coeffs = jnp.where(live, coeffs, jnp.zeros_like(coeffs))
+        fixed[...] = jnp.dot(sb[...], coeffs, preferred_element_type=F32)
+
+    @pl.when(g > 0)
+    def _():
+        loads[2].wait()
+        c_full = c_in[...].T
+        high = c_full.astype(BF16)
+        c_hi[...] = high
+        c_lo[...] = (c_full - high.astype(F32)).astype(BF16)
+        local_work()
 
     owner_only(s, chain)
 
-    loads[6].wait()
-    loads[7].wait()
-    coeffs = sc[...]
-    live = lax.broadcasted_iota(jnp.int32, coeffs.shape, 0) < width_ref[0, 0]
-    coeffs = jnp.where(live, coeffs, jnp.zeros_like(coeffs))
-    fixed[...] = jnp.dot(sb[...], coeffs, preferred_element_type=F32)
+    @pl.when(g == 0)
+    def _():
+        loads[2].wait()
+        local_work()
 
     def gather_wait(src):
         remote(v_all.at[src], v_all.at[src], gat_send.at[0], gat_recv.at[src], g, src).wait_recv()
@@ -215,11 +259,8 @@
         nb_copies.append(remote(cand.at[2], cand.at[o], nb_send.at[i], nb_recv.at[i], g, t))
     for copy in nb_copies:
         copy.start()
-    stores = [pltpu.make_async_copy(cand.at[2], block_out.at[0, 0], out_sem.at[chunks])]
-    stores[0].start()
-    top_stage[...] = v.astype(F32).T
-    stores.append(pltpu.make_async_copy(top_stage, top_out.at[0], out_sem.at[chunks + 1]))
-    stores[1].start()
+    block_out[0, 0] = cand[2]
+    top_out[0] = v.astype(F32).T
     loads[8].wait()
     for copy in nb_copies:
         copy.wait_recv()
@@ -230,17 +271,21 @@
     for i in range(chunks):
         here = slice(i * step, (i + 1) * step)
         bound = jnp.dot(cm[here, :], linked[...], preferred_element_type=F32)
-        result[i] = (fixed[here, :] + bound).astype(BF16)
-        store = pltpu.make_async_copy(result.at[i], interior_out.at[0, 0, pl.ds(i * step, step)], out_sem.at[i])
-        store.start()
-        stores.append(store)
+        interior_out[0, 0, here, :] = (fixed[here, :] + bound).astype(BF16)
 
     for d in range(1, subs):
         t = peer(d)
         owner_only(t, lambda t=t: piece_copy(t).wait_send())
 
+    if groups > 1:
+        @pl.when(g == 0)
+        def _():
+            for d in range(subs):
+                t = peer(d)
+                owner_only(t, lambda t=t: ahead_copy(t).wait_send())
+
     def sent():
-        @pl.when(g < groups - 1)
+        @pl.when((g > 0) & (g < groups - 1))
         def _():
             hop_copy().wait_send()
 
@@ -250,8 +295,6 @@
     owner_only(s, sent)
     for copy in nb_copies:
         copy.wait_send()
-    for store in stores:
-        store.wait()
 
 
 def hand_over_kernel(top, block, interior, top_out, block_out, interior_out, sem):
@@ -330,6 +373,9 @@
         dma((owners,)),
         dma((4,)),
         dma((4,)),
+        vmem((subs, cols, lane_rows), F32),
+        dma((owners,)),
+        dma((subs,)),
     ]
     results = pl.pallas_call(
         functools.partial(kernel, groups, subs, owners),
@@ -339,7 +385,7 @@
             jax.ShapeDtypeStruct((1, 1, ni, modes), BF16),
         ),
         in_specs=[hbm, hbm, hbm, hbm, hbm, hbm, hbm, hbm, smem, hbm, smem],
-        out_specs=(hbm, hbm, hbm),
+        out_specs=(pl.BlockSpec(memory_space=pltpu.VMEM),) * 3,
         scratch_shapes=scratch,
         compiler_params=pltpu.CompilerParams(
             collective_id=0, has_side_effects=True, vmem_limit_bytes=24 * 1024 * 1024

time: 27 us -> 24.6 us (0.911)
  Pallas kernels: 24.9 us -> 22.4 us
    pallas_call x1, Pallas kernels: 24 us -> 21.5 us  [body(): pl.pallas_call(functools.partial(kernel, groups, subs, owners), out_shape...]
where the time goes in v3:
time: 24.6 us; the launch traced here: 24.3 us
  Pallas kernels  22.4 us (91%)
  between operations  1.3 us (5%)
  local copies, waits for them, and re-layouts  0.65 us (3%)
    pallas_call x1, Pallas kernels, body(): pl.pallas_call(functools.partial(kernel, groups, subs, owners), out_shape...  21.5 us
    pallas_call x1, Pallas kernels, hand_over(): pl.pallas_call(hand_over_kernel, out_shape=tuple((jax.ShapeDtypeStruct(r....  0.88 us
    unnamed x2, local copies, waits for them, and re-layouts  0.65 us

profile of v3, /device:TPU:24, one launch (start us, length us, event | category | flops | bytes accessed | tf_op | source)
XLA Modules:
  0.0 24.3 jit_solution(5424939811532931534)
XLA Ops:
  1.3 0.0 copy-start
  1.3 0.6 %copy-done = s32[1,1,4]{2,1,0:T(1,128)S(1)} copy-done((s32[1,1,4]{2,1,0:T(1,128)S(1)}, s32[1,1,4]{2,1,0:T(1,128)}, u32[]{:S(2)}) %copy-start) | copy-done | bytes 40
  1.9 21.5 %shard_map.130 = (f32[1,512,128]{2,1,0:T(8,128)S(1)}, bf16[1,1,128,128]{3,2,1,0:T(8,128)(2,1)S(1)}, bf16[1,1,1536,128]{3,2,1,0:T(8,128)(2,1)S(1)}) custom-call(bf16[1,64,256]{2,1,0:T(8,128)(2,1)} %tb_hbm.1, bf16[1,256,128]{2,1,0:T(8,128)(2,1)} %tc_hbm.1, f32[1,512,512]{2,1,0:T(8,128)} %c_hbm.1, f32[1,1,128,512]{3,2,1,0:T(8,128)} %bc_hbm.1, ...), custom_call_target="tpu_custom_call" | custom-call | flops 500000000 | bytes 5000000 | tf_op jit(solution)/shard_map/pallas_call | solution.py:380
  23.5 0.9 %shard_map.131 = (f32[1,512,128]{2,1,0:T(8,128)}, bf16[1,1,128,128]{3,2,1,0:T(8,128)(2,1)}, bf16[1,1,1536,128]{3,2,1,0:T(8,128)(2,1)}) custom-call(f32[1,512,128]{2,1,0:T(8,128)S(1)} %get-tuple-element.6.top, bf16[1,1,128,128]{3,2,1,0:T(8,128)(2,1)S(1)} %get-tuple-element.7.block, bf16[1,1,1536,128]{3,2,1,0:T(8,128)(2,1)S(1)} %get-tuple-element.8.interior), custom_call_target="tpu_custom_call" | custom-call | tf_op jit(solution)/shard_map/pallas_call | solution.py:316
Async XLA Ops:
  1.3 0.7 %copy-start = (s32[1,1,4]{2,1,0:T(1,128)S(1)}, s32[1,1,4]{2,1,0:T(1,128)}, u32[]{:S(2)}) copy-start(s32[1,1,4]{2,1,0:T(1,128)} %adj_ref.1) | copy-start | bytes 52

commit v4 on v3

--- a/solution.py
+++ b/solution.py
@@ -29,7 +29,7 @@
     sc_hbm,
     width_ref,
     cm_hbm,
-    adj_ref,
+    adj_hbm,
     top_out,
     block_out,
     interior_out,
@@ -69,6 +69,7 @@
     gathered_before,
     ahead_send,
     ahead_recv,
+    adj_ref,
 ):
     g = lax.axis_index("grp")
     s = lax.axis_index("sub")
@@ -89,6 +90,7 @@
         pltpu.make_async_copy(sb_hbm.at[0, 0], sb, in_sem.at[6]),
         pltpu.make_async_copy(sc_hbm.at[0, 0], sc, in_sem.at[7]),
         pltpu.make_async_copy(cm_hbm.at[0, 0], cm, in_sem.at[8]),
+        pltpu.make_async_copy(adj_hbm, adj_ref, in_sem.at[9]),
     ]
     for load in loads:
         load.start()
@@ -262,6 +264,7 @@
     block_out[0, 0] = cand[2]
     top_out[0] = v.astype(F32).T
     loads[8].wait()
+    loads[9].wait()
     for copy in nb_copies:
         copy.wait_recv()
     size = cand.shape[1]
@@ -336,7 +339,6 @@
     slots = adj.shape[2]
     chunks = 4
     hbm = pl.BlockSpec(memory_space=pl.ANY)
-    smem = pl.BlockSpec(memory_space=pltpu.SMEM)
     dma = pltpu.SemaphoreType.DMA
     vmem = pltpu.VMEM
     scratch = [
@@ -363,7 +365,7 @@
         vmem((5, nb, modes), BF16),
         vmem((slots * nb, modes), BF16),
         vmem((chunks, ni // chunks, modes), BF16),
-        dma((9,)),
+        dma((10,)),
         dma((chunks + 2,)),
         dma((owners,)),
         dma((subs,)),
@@ -376,6 +378,7 @@
         vmem((subs, cols, lane_rows), F32),
         dma((owners,)),
         dma((subs,)),
+        pltpu.SMEM(adj.shape, jnp.int32),
     ]
     results = pl.pallas_call(
         functools.partial(kernel, groups, subs, owners),
@@ -384,14 +387,14 @@
             jax.ShapeDtypeStruct((1, 1, nb, modes), BF16),
             jax.ShapeDtypeStruct((1, 1, ni, modes), BF16),
         ),
-        in_specs=[hbm, hbm, hbm, hbm, hbm, hbm, hbm, hbm, smem, hbm, smem],
+        in_specs=[hbm, hbm, hbm, hbm, hbm, hbm, hbm, hbm, pl.BlockSpec(memory_space=pltpu.SMEM), hbm, hbm],
         out_specs=(pl.BlockSpec(memory_space=pltpu.VMEM),) * 3,
         scratch_shapes=scratch,
         compiler_params=pltpu.CompilerParams(
             collective_id=0, has_side_effects=True, vmem_limit_bytes=24 * 1024 * 1024
         ),
         cost_estimate=pl.CostEstimate(flops=500_000_000, bytes_accessed=5_000_000, transcendentals=0),
-    )(*[pltpu.with_memory_space_constraint(a, pltpu.HBM) if a.ndim > 2 and a.dtype != jnp.int32 else a for a in args])
+    )(*[pltpu.with_memory_space_constraint(a, pltpu.HBM) if a.ndim > 2 else a for a in args])
     return hand_over(results)
 
 

time: 24.6 us -> 23.4 us (0.951)
  local copies, waits for them, and re-layouts: 0.65 us -> 0 us
  Pallas kernels: 22.4 us -> 21.9 us
    unnamed x2 -> x0, local copies, waits for them, and re-layouts: 0.65 us -> none
    pallas_call x1, Pallas kernels: 21.5 us -> 21 us  [body(): pl.pallas_call(functools.partial(kernel, groups, subs, owners), out_shape...]
where the time goes in v4:
time: 23.4 us; the launch traced here: 23.2 us
  Pallas kernels  21.9 us (94%)
  between operations  1.29 us (6%)
    pallas_call x1, Pallas kernels, body(): pl.pallas_call(functools.partial(kernel, groups, subs, owners), out_shape...  21 us
    pallas_call x1, Pallas kernels, hand_over(): pl.pallas_call(hand_over_kernel, out_shape=tuple((jax.ShapeDtypeStruct(r....  0.88 us

profile of v4, /device:TPU:24, one launch (start us, length us, event | category | flops | bytes accessed | tf_op | source)
XLA Modules:
  0.0 23.2 jit_solution(8232413419271034596)
XLA Ops:
  1.3 21.0 %shard_map.130 = (f32[1,512,128]{2,1,0:T(8,128)S(1)}, bf16[1,1,128,128]{3,2,1,0:T(8,128)(2,1)S(1)}, bf16[1,1,1536,128]{3,2,1,0:T(8,128)(2,1)S(1)}) custom-call(bf16[1,64,256]{2,1,0:T(8,128)(2,1)} %tb_hbm.1, bf16[1,256,128]{2,1,0:T(8,128)(2,1)} %tc_hbm.1, f32[1,512,512]{2,1,0:T(8,128)} %c_hbm.1, f32[1,1,128,512]{3,2,1,0:T(8,128)} %bc_hbm.1, ...), custom_call_target="tpu_custom_call" | custom-call | flops 500000000 | bytes 5000000 | tf_op jit(solution)/shard_map/pallas_call | solution.py:383
  22.3 0.9 %shard_map.131 = (f32[1,512,128]{2,1,0:T(8,128)}, bf16[1,1,128,128]{3,2,1,0:T(8,128)(2,1)}, bf16[1,1,1536,128]{3,2,1,0:T(8,128)(2,1)}) custom-call(f32[1,512,128]{2,1,0:T(8,128)S(1)} %get-tuple-element.6.top, bf16[1,1,128,128]{3,2,1,0:T(8,128)(2,1)S(1)} %get-tuple-element.7.block, bf16[1,1,1536,128]{3,2,1,0:T(8,128)(2,1)S(1)} %get-tuple-element.8.interior), custom_call_target="tpu_custom_call" | custom-call | tf_op jit(solution)/shard_map/pallas_call | solution.py:319
